TPU v7x, 32 devices: a whole 2x2x4 slice. The times are simulated.
32 devices in a mesh: dp: 16 (over z, y, core), fsdp: 2 (over x).
Axes of the slice: x: 2, y: 2, z: 4, core: 2. Of those that a mesh axis runs over, the one named last changes fastest.
Arguments:
- tokens: bfloat16 [128, 256, 384], P(('dp', 'fsdp')), may hold values from -6 to 6
- condition: bfloat16 [128, 384], P(('dp', 'fsdp')), may hold values from -6 to 6
- image_grid: int32 [128, 2], P(('dp', 'fsdp')), may hold values from 12 to 20, as said below
- image_counts: int32 [32], P(('dp', 'fsdp')), may hold values from 1 to 4, as said below
- cotangent: bfloat16 [128, 256, 384], P(('dp', 'fsdp')), may hold values from -6 to 6
- entry_master: float32 [2, 384, 5376], P(None, 'fsdp'), as said below
- exit_master: float32 [2, 1536, 384], P(None, 'fsdp'), may hold values from -0.15625 to 0.15625
- bias_master: float32 [2, 5760], P(None, 'fsdp'), may hold values from -0.6 to 0.6
- entry_moment: float32 [2, 384, 5376], P(None, 'fsdp'), may hold values from -6 to 6
- exit_moment: float32 [2, 1536, 384], P(None, 'fsdp'), may hold values from -6 to 6
- bias_moment: float32 [2, 5760], P(None, 'fsdp'), may hold values from -6 to 6
- entry_square: float32 [2, 384, 5376], P(None, 'fsdp'), may hold values from 0.3 to 3
- exit_square: float32 [2, 1536, 384], P(None, 'fsdp'), may hold values from 0.3 to 3
- bias_square: float32 [2, 5760], P(None, 'fsdp'), may hold values from 0.3 to 3
Outputs:
- block_output: bfloat16 [128, 256, 384], P(('dp', 'fsdp'))
- grad_tokens: float32 [128, 256, 384], P(('dp', 'fsdp'))
- grad_condition: float32 [128, 384], P(('dp', 'fsdp'))
- entry_grad: float32 [2, 384, 5376], P(None, 'fsdp')
- entry_moment_new: float32 [2, 384, 5376], P(None, 'fsdp')
- entry_square_new: float32 [2, 384, 5376], P(None, 'fsdp')
- entry_master_new: float32 [2, 384, 5376], P(None, 'fsdp')
- entry_weight: bfloat16 [2, 384, 5376], P(None, 'fsdp')
- exit_grad: float32 [2, 1536, 384], P(None, 'fsdp')
- exit_moment_new: float32 [2, 1536, 384], P(None, 'fsdp')
- exit_square_new: float32 [2, 1536, 384], P(None, 'fsdp')
- exit_master_new: float32 [2, 1536, 384], P(None, 'fsdp')
- exit_weight: bfloat16 [2, 1536, 384], P(None, 'fsdp')
- bias_grad: float32 [2, 5760], P(None, 'fsdp')
- bias_moment_new: float32 [2, 5760], P(None, 'fsdp')
- bias_square_new: float32 [2, 5760], P(None, 'fsdp')
- bias_master_new: float32 [2, 5760], P(None, 'fsdp')
- bias_weight: bfloat16 [2, 5760], P(None, 'fsdp')
- exit_bias_grad: float32 [2, 384], P(None, 'fsdp')
Inputs may be any that keep to these rules, and one draw needn't show every extreme that they name: `image_grid`: each image has 12 to 20 patch rows and columns and rows times columns at most 256; its patches take the first rows times columns slots. In every draw some image fills all 256 slots and some has 20 rows. `image_counts`: image slot j of a device is live when j is below the device's count; some device holds 4 live images and some holds one. `entry_master`: packed weights of each block.
All inputs are finite; a program needn't handle non-finite values.
Results may differ from a plain program's by a relative error of at most 0.018.
The roundings to bfloat16 on the way count: a program that leaves them out, or rounds other values in their place, can miss the bound.
Values may be sent and summed in bfloat16 or wider, within the bound.
No kernel may reach another device: no remote copies, remote signals or barrier semaphores. Data moves between devices by JAX's collectives and lax.ppermute only.
A program may use at most 256 MiB of HBM per device.

v0:
```python
from functools import partial
import jax
import jax.numpy as jnp
from jax import lax
from jax.sharding import PartitionSpec as P

D = 384
HEADS = 6
HEAD_DIM = 64
FF = 1536
LAYERS = 2
IMG_DEV = 4
STEP = 4
SLOTS = 256
eps_norm = 1e-06
neg_big = -1e30
beta_one = 0.5
beta_two = 0.6
adam_eps = 1e-08
learn_rate = 0.02
decay_rate = 0.1


def matmul(left, right):
    return jnp.dot(left, right, preferred_element_type=jnp.float32)


def normalize(values):
    row_mean = jnp.mean(values, axis=-1, keepdims=True)
    centered = values - row_mean
    variance = jnp.mean(centered * centered, axis=-1, keepdims=True)
    return centered * lax.rsqrt(variance + eps_norm)


def modulate(values, offset, scaling):
    return normalize(values) * (1.0 + scaling[:, None, :]) + offset[:, None, :]


def adam_update(gradient, master, moment, square):
    new_moment = beta_one * moment + (1.0 - beta_one) * gradient
    new_square = beta_two * square + (1.0 - beta_two) * gradient * gradient
    first_fix = 1.0 - beta_one**STEP
    second_fix = 1.0 - beta_two**STEP
    direction = (
        new_moment / first_fix / (jnp.sqrt(new_square / second_fix) + adam_eps)
        + decay_rate * master
    )
    new_master = master - learn_rate * direction
    return (new_moment, new_square, new_master)


def reduce_grads(grad_entry, grad_exit, grad_bias, grad_tail):
    owner_grads = (
        lax.psum_scatter(grad_entry, "fsdp", scatter_dimension=1, tiled=True),
        lax.psum_scatter(grad_exit, "fsdp", scatter_dimension=1, tiled=True),
        lax.psum_scatter(grad_bias, "fsdp", scatter_dimension=1, tiled=True),
        lax.psum_scatter(grad_tail, "fsdp", scatter_dimension=1, tiled=True),
    )
    summed = lax.psum((owner_grads[0], owner_grads[1], owner_grads[2], owner_grads[3]), "dp")
    return (summed[0], summed[1], summed[2], summed[3])


def block_forward(residual, live_mask, cond_act, entry_weights, exit_weights, bias_low):
    images = residual.shape[0]
    row_count = images * SLOTS
    query_end = 3 * D
    proj_end = 4 * D
    hidden_end = 4 * D + FF
    ada_end = 10 * D + FF
    bias_all = bias_low.astype(jnp.float32)
    modulation = (
        matmul(cond_act, entry_weights[:, hidden_end:ada_end]) + bias_all[hidden_end:ada_end]
    )
    mod_parts = jnp.split(modulation, 6, axis=-1)
    normed_one = (
        modulate(residual, mod_parts[0], mod_parts[1]).astype(jnp.bfloat16).reshape(row_count, D)
    )
    projected = (matmul(normed_one, entry_weights[:, :query_end]) + bias_all[:query_end]).astype(
        jnp.bfloat16
    )
    projected = projected.reshape(images, SLOTS, 3, HEADS, HEAD_DIM)
    queries = projected[:, :, 0]
    keys_all = projected[:, :, 1]
    values_all = projected[:, :, 2]
    scores = jnp.einsum(
        "gqhd,gkhd->ghqk", queries, keys_all, preferred_element_type=jnp.float32
    ) * HEAD_DIM ** (-0.5)
    scores = jnp.where(live_mask[:, None, None, :], scores, neg_big)
    row_max = jnp.max(scores, axis=-1, keepdims=True)
    exponent = jnp.exp(scores - row_max)
    row_total = jnp.sum(exponent, axis=-1, keepdims=True)
    weights_soft = exponent / row_total
    weights_low = weights_soft.astype(jnp.bfloat16)
    attended = jnp.einsum(
        "ghqk,gkhd->gqhd", weights_low, values_all, preferred_element_type=jnp.float32
    )
    attended = attended.astype(jnp.bfloat16).reshape(row_count, D)
    branch = matmul(attended, entry_weights[:, query_end:proj_end]) + bias_all[query_end:proj_end]
    branch = branch.reshape(images, SLOTS, D)
    middle = residual + mod_parts[2][:, None, :] * branch
    normed_two = (
        modulate(middle, mod_parts[3], mod_parts[4]).astype(jnp.bfloat16).reshape(row_count, D)
    )
    pre_act = (
        matmul(normed_two, entry_weights[:, proj_end:hidden_end]) + bias_all[proj_end:hidden_end]
    )
    activated = jax.nn.gelu(pre_act, approximate=True).astype(jnp.bfloat16)
    leaving = (matmul(activated, exit_weights) + bias_all[ada_end:]).reshape(images, SLOTS, D)
    output = middle + mod_parts[5][:, None, :] * leaving
    saved = (
        mod_parts,
        normed_one,
        queries,
        keys_all,
        values_all,
        weights_soft,
        weights_low,
        attended,
        branch,
        middle,
        normed_two,
        pre_act,
        activated,
        leaving,
    )
    return (output, saved)


def block_backward(
    residual, live_mask, cond_act, entry_weights, exit_weights, bias_low, grad_output
):
    images = residual.shape[0]
    row_count = images * SLOTS
    query_end = 3 * D
    proj_end = 4 * D
    hidden_end = 4 * D + FF
    ada_end = 10 * D + FF
    output, saved = block_forward(
        residual, live_mask, cond_act, entry_weights, exit_weights, bias_low
    )
    (
        mod_parts,
        normed_one,
        queries,
        keys_all,
        values_all,
        weights_soft,
        weights_low,
        attended,
        branch,
        middle,
        normed_two,
        pre_act,
        activated,
        leaving,
    ) = saved
    grad_leaving = (
        (mod_parts[5][:, None, :] * grad_output).astype(jnp.bfloat16).reshape(row_count, D)
    )
    grad_gate_two = jnp.sum(grad_output * leaving, axis=1)
    grad_exit = matmul(activated.T, grad_leaving)
    grad_bias_exit = jnp.sum(grad_leaving.astype(jnp.float32), axis=0)
    grad_activated = matmul(grad_leaving, exit_weights.T)
    gelu_out, gelu_pull = jax.vjp(partial(jax.nn.gelu, approximate=True), pre_act)
    grad_pre = gelu_pull(grad_activated)[0].astype(jnp.bfloat16)
    grad_fc_in = matmul(normed_two.T, grad_pre)
    grad_bias_fc = jnp.sum(grad_pre.astype(jnp.float32), axis=0)
    grad_normed_two = matmul(grad_pre, entry_weights[:, proj_end:hidden_end].T).reshape(
        images, SLOTS, D
    )
    second_out, second_pull = jax.vjp(modulate, middle, mod_parts[3], mod_parts[4])
    grad_mid_norm, grad_shift_two, grad_scale_two = second_pull(grad_normed_two)
    grad_middle = grad_output + grad_mid_norm
    grad_branch = (
        (mod_parts[2][:, None, :] * grad_middle).astype(jnp.bfloat16).reshape(row_count, D)
    )
    grad_gate_one = jnp.sum(grad_middle * branch, axis=1)
    grad_proj = matmul(attended.T, grad_branch)
    grad_bias_proj = jnp.sum(grad_branch.astype(jnp.float32), axis=0)
    grad_attended = matmul(grad_branch, entry_weights[:, query_end:proj_end].T).astype(jnp.bfloat16)
    grad_attended = grad_attended.reshape(images, SLOTS, HEADS, HEAD_DIM)
    grad_values = jnp.einsum(
        "ghqk,gqhd->gkhd", weights_low, grad_attended, preferred_element_type=jnp.float32
    )
    grad_weights = jnp.einsum(
        "gqhd,gkhd->ghqk", grad_attended, values_all, preferred_element_type=jnp.float32
    )
    grad_scores = weights_soft * (
        grad_weights - jnp.sum(grad_weights * weights_soft, axis=-1, keepdims=True)
    )
    grad_scores = jnp.where(live_mask[:, None, None, :], grad_scores, 0.0).astype(
        jnp.bfloat16
    ) * HEAD_DIM ** (-0.5)
    grad_queries = jnp.einsum(
        "ghqk,gkhd->gqhd", grad_scores, keys_all, preferred_element_type=jnp.float32
    )
    grad_keys = jnp.einsum(
        "ghqk,gqhd->gkhd", grad_scores, queries, preferred_element_type=jnp.float32
    )
    grad_projected = (
        jnp.stack([grad_queries, grad_keys, grad_values], axis=2)
        .astype(jnp.bfloat16)
        .reshape(row_count, 3 * D)
    )
    grad_query_in = matmul(normed_one.T, grad_projected)
    grad_bias_query = jnp.sum(grad_projected.astype(jnp.float32), axis=0)
    grad_normed_one = matmul(grad_projected, entry_weights[:, :query_end].T).reshape(
        images, SLOTS, D
    )
    first_out, first_pull = jax.vjp(modulate, residual, mod_parts[0], mod_parts[1])
    grad_in_norm, grad_shift_one, grad_scale_one = first_pull(grad_normed_one)
    grad_residual = grad_middle + grad_in_norm
    grad_modulation = jnp.concatenate(
        [
            grad_shift_one,
            grad_scale_one,
            grad_gate_one,
            grad_shift_two,
            grad_scale_two,
            grad_gate_two,
        ],
        axis=-1,
    ).astype(jnp.bfloat16)
    grad_ada = matmul(cond_act.T, grad_modulation)
    grad_bias_ada = jnp.sum(grad_modulation.astype(jnp.float32), axis=0)
    grad_cond_act = matmul(grad_modulation, entry_weights[:, hidden_end:ada_end].T)
    grad_entry = jnp.concatenate([grad_query_in, grad_proj, grad_fc_in, grad_ada], axis=1)
    grad_bias = jnp.concatenate(
        [grad_bias_query, grad_bias_proj, grad_bias_fc, grad_bias_ada, grad_bias_exit]
    )
    return (grad_residual, grad_cond_act, grad_entry, grad_exit, grad_bias)


def per_device(
    tokens,
    condition,
    image_grid,
    image_counts,
    cotangent,
    entry_master,
    exit_master,
    bias_master,
    entry_moment,
    exit_moment,
    bias_moment,
    entry_square,
    exit_square,
    bias_square,
):
    live_image = jnp.arange(IMG_DEV) < image_counts[0]
    cell_count = image_grid[:, 0] * image_grid[:, 1]
    live_mask = jnp.logical_and(
        live_image[:, None], jnp.arange(SLOTS)[None, :] < cell_count[:, None]
    )
    cond_float = condition.astype(jnp.float32)
    cond_act = jax.nn.silu(cond_float).astype(jnp.bfloat16)
    fetched = []
    inputs_kept = []
    residual = tokens.astype(jnp.float32)
    for layer_index in range(LAYERS):
        gathered = (
            lax.all_gather(
                entry_master[layer_index].astype(jnp.bfloat16), "fsdp", axis=0, tiled=True
            ),
            lax.all_gather(
                exit_master[layer_index].astype(jnp.bfloat16), "fsdp", axis=0, tiled=True
            ),
            lax.all_gather(
                bias_master[layer_index].astype(jnp.bfloat16), "fsdp", axis=0, tiled=True
            ),
        )
        fetched.append(gathered)
        inputs_kept.append(residual)
        residual = block_forward(
            residual, live_mask, cond_act, gathered[0], gathered[1], gathered[2]
        )[0]
    block_output = residual.astype(jnp.bfloat16)
    grad_residual = cotangent.astype(jnp.float32) * live_mask[..., None].astype(jnp.float32)
    grad_cond_sum = jnp.zeros_like(cond_float)
    summed_layers = []
    for layer_index in reversed(range(LAYERS)):
        gathered = (
            lax.all_gather(
                entry_master[layer_index].astype(jnp.bfloat16), "fsdp", axis=0, tiled=True
            ),
            lax.all_gather(
                exit_master[layer_index].astype(jnp.bfloat16), "fsdp", axis=0, tiled=True
            ),
            lax.all_gather(
                bias_master[layer_index].astype(jnp.bfloat16), "fsdp", axis=0, tiled=True
            ),
        )
        grad_residual, grad_cond_act, grad_entry, grad_exit, grad_bias = block_backward(
            inputs_kept[layer_index],
            live_mask,
            cond_act,
            gathered[0],
            gathered[1],
            gathered[2],
            grad_residual,
        )
        grad_cond_sum = grad_cond_sum + grad_cond_act
        tail_start = grad_bias.shape[0] - D
        summed_layers.insert(
            0,
            reduce_grads(
                grad_entry[None], grad_exit[None], grad_bias[None], grad_bias[None, tail_start:]
            ),
        )
    summed_groups = (
        jnp.concatenate([summed_one[0] for summed_one in summed_layers], axis=0),
        jnp.concatenate([summed_one[1] for summed_one in summed_layers], axis=0),
        jnp.concatenate([summed_one[2] for summed_one in summed_layers], axis=0),
        jnp.concatenate([summed_one[3] for summed_one in summed_layers], axis=0),
    )
    silu_out, silu_pull = jax.vjp(jax.nn.silu, cond_float)
    grad_condition = silu_pull(grad_cond_sum)[0]
    scale_grad = (IMG_DEV * SLOTS * lax.axis_size("dp") * lax.axis_size("fsdp")) ** (-0.5)
    entry_grad = summed_groups[0] * scale_grad
    exit_grad = summed_groups[1] * scale_grad
    bias_grad = summed_groups[2] * scale_grad
    exit_bias_grad = summed_groups[3] * scale_grad
    entry_moment_new, entry_square_new, entry_master_new = adam_update(
        entry_grad, entry_master, entry_moment, entry_square
    )
    exit_moment_new, exit_square_new, exit_master_new = adam_update(
        exit_grad, exit_master, exit_moment, exit_square
    )
    bias_moment_new, bias_square_new, bias_master_new = adam_update(
        bias_grad, bias_master, bias_moment, bias_square
    )
    return (
        block_output,
        grad_residual,
        grad_condition,
        entry_grad,
        entry_moment_new,
        entry_square_new,
        entry_master_new,
        entry_master_new.astype(jnp.bfloat16),
        exit_grad,
        exit_moment_new,
        exit_square_new,
        exit_master_new,
        exit_master_new.astype(jnp.bfloat16),
        bias_grad,
        bias_moment_new,
        bias_square_new,
        bias_master_new,
        bias_master_new.astype(jnp.bfloat16),
        exit_bias_grad,
    )


def solution(mesh):
    return jax.shard_map(
        per_device,
        mesh=mesh,
        in_specs=(
            P(("dp", "fsdp"), None, None),
            P(("dp", "fsdp"), None),
            P(("dp", "fsdp"), None),
            P(("dp", "fsdp")),
            P(("dp", "fsdp"), None, None),
            P(None, "fsdp", None),
            P(None, "fsdp", None),
            P(None, "fsdp"),
            P(None, "fsdp", None),
            P(None, "fsdp", None),
            P(None, "fsdp"),
            P(None, "fsdp", None),
            P(None, "fsdp", None),
            P(None, "fsdp"),
        ),
        out_specs=(
            P(("dp", "fsdp"), None, None),
            P(("dp", "fsdp"), None, None),
            P(("dp", "fsdp"), None),
            P(None, "fsdp", None),
            P(None, "fsdp", None),
            P(None, "fsdp", None),
            P(None, "fsdp", None),
            P(None, "fsdp", None),
            P(None, "fsdp", None),
            P(None, "fsdp", None),
            P(None, "fsdp", None),
            P(None, "fsdp", None),
            P(None, "fsdp", None),
            P(None, "fsdp"),
            P(None, "fsdp"),
            P(None, "fsdp"),
            P(None, "fsdp"),
            P(None, "fsdp"),
            P(None, "fsdp"),
        ),
        check_vma=False,
    )
```

profile of v0, /device:TPU:0, one launch (start us, length us, event | category | flops | bytes accessed | tf_op | source)
XLA Modules:
  0.0 899.9 jit_solution(8270326126173067755)
XLA Ops:
  7.2 3.8 convert.48
  11.0 2.2 fusion.203
  18.9 9.8 %all-reduce.4 = (bf16[5760]{0:T(1024)(128)(2,1)S(1)}, bf16[5760]{0:T(1024)(128)(2,1)S(1)}) all-reduce(bf16[5760]{0:T(1024)(128)(2,1)S(1)} %dynamic-update-slice, bf16[5760]{0:T(1024)(128)(2,1)S(1)} %dynamic-update-slice.1), channel_id=3, replica_groups=mesh['dp'=16,'fsdp'=2] {'fsdp'}, use_global_device_ids=true, to_apply=%add | all-reduce | flops 11520 | bytes 46080
  30.4 41.8 %all-gather.11.cloned.1.call-done = bf16[1,384,5376]{2,1,0:T(8,128)(2,1)} async-done(((bf16[1,192,5376]{2,1,0:T(8,128)(2,1)}), bf16[1,384,5376]{2,1,0:T(8,128)(2,1)}) %all-gather.11.cloned.1.call-update) | async-done | bytes 4128784 | tf_op jit(solution)/shard_map/all_gather | solution.py:262
  74.1 56.3 %all-gather.15.cloned.1.call-done = bf16[1,384,5376]{2,1,0:T(8,128)(2,1)} async-done(((bf16[1,192,5376]{2,1,0:T(8,128)(2,1)}), bf16[1,384,5376]{2,1,0:T(8,128)(2,1)}) %all-gather.15.cloned.1.call-update) | async-done | bytes 4128784 | tf_op jit(solution)/shard_map/all_gather | solution.py:262
  133.6 4.0 fusion.26
  137.6 4.3 copy.117
  142.0 5.6 reshape.370
  147.6 2.4 fusion.205
  151.1 2.3 fusion.209
  154.0 2.1 copy-done.77
  156.9 1.9 convolution_add_fusion.5
  161.2 6.9 multiply_convert_fusion.1
  168.1 4.0 convolution_add_fusion.7
  173.8 2.1 convert_reduce_fusion.5
  176.9 4.0 fusion.27
  180.9 4.3 copy.123
  185.2 5.6 reshape.376
  190.8 2.4 fusion.204
  195.4 2.3 fusion.210
  198.4 2.1 copy-done.78
  205.8 6.5 multiply_convert_fusion
  214.0 3.3 convolution_bitcast_fusion
  217.4 7.5 convert_reduce_fusion
  224.9 4.1 fusion.134
  233.1 1.9 add_add_fusion.3
  236.6 2.0 convert_reduce_fusion.6
  239.6 2.5 convolution_convert_fusion.1
  242.1 2.3 copy.129
  244.4 3.0 reshape.384
  247.4 5.1 fusion.152
  252.5 11.4 %fusion.95 = bf16[4,256,1,6,64]{1,4,3,0,2:T(8,128)(2,1)} fusion(f32[4,6,256,256]{2,3,1,0:T(8,128)} %fusion.152, pred[4,256]{1,0:T(4,128)(4,1)S(1)} %get-tuple-element.115, bf16[4,256,1,6,64]{1,0,4,3,2:T(4,128)(2,1)} %copy-done.34, f32[4,6,256,256]{2,3,1,0:T(8,128)} %copy-done.78, f32[4,6,256]{2,1,0:T(8,128)S(1)} %get-tuple-element.120), kind=kOutput, calls=%fused_computation.151 | convolution fusion | flops 218634496 | bytes 14181376 | tf_op jit(solution)/shard_map/ghqk,gkhd->gqhd/dot_general | solution.py:194
  264.0 11.5 %fusion.100 = bf16[4,256,1,6,64]{1,4,3,0,2:T(8,128)(2,1)} fusion(f32[4,6,256,256]{2,3,1,0:T(8,128)} %fusion.152, pred[4,256]{1,0:T(4,128)(4,1)S(1)} %get-tuple-element.115, bf16[4,256,1,6,64]{1,0,4,3,2:T(4,128)(2,1)} %copy-done.33, f32[4,6,256,256]{2,3,1,0:T(8,128)} %copy-done.78, f32[4,6,256]{2,1,0:T(8,128)S(1)} %get-tuple-element.120), kind=kOutput, calls=%fused_computation.152 | convolution fusion | flops 218634496 | bytes 14181376 | tf_op jit(solution)/shard_map/ghqk,gqhd->gkhd/dot_general | solution.py:197
  275.5 4.2 fusion.92
  281.5 3.1 multiply_reduce_fusion.8
  286.6 2.4 multiply_reduce_fusion.4
  289.9 3.3 convolution_bitcast_fusion.1
  293.4 3.7 copy.147
  303.5 3.6 maximum_bitcast_fusion.1
  308.2 7.7 convert_reduce_fusion.1
  316.0 4.0 fusion.138
  327.7 3.7 fusion.150
  331.4 10.5 %fusion.105 = bf16[4,256,1,6,64]{1,4,3,0,2:T(8,128)(2,1)S(1)} fusion(f32[4,6,256,256]{2,3,1,0:T(8,128)} %fusion.150, pred[4,256]{1,0:T(4,128)(4,1)S(1)} %get-tuple-element.115, bf16[4,256,1,6,64]{1,0,4,3,2:T(4,128)(2,1)S(1)} %copy-done.30, f32[4,6,256,256]{2,3,1,0:T(8,128)} %copy-done.77, f32[4,6,256]{2,1,0:T(8,128)S(1)} %copy-done.80), kind=kOutput, calls=%fused_computation.153 | convolution fusion | flops 218634496 | bytes 14181376 | tf_op jit(solution)/shard_map/ghqk,gkhd->gqhd/dot_general | solution.py:194
  341.9 11.6 %fusion.110 = bf16[4,256,1,6,64]{1,4,3,0,2:T(8,128)(2,1)} fusion(f32[4,6,256,256]{2,3,1,0:T(8,128)} %fusion.150, pred[4,256]{1,0:T(4,128)(4,1)S(1)} %get-tuple-element.115, bf16[4,256,1,6,64]{1,0,4,3,2:T(4,128)(2,1)S(1)} %copy-done.28, f32[4,6,256,256]{2,3,1,0:T(8,128)} %copy-done.77, f32[4,6,256]{2,1,0:T(8,128)S(1)} %copy-done.80), kind=kOutput, calls=%fused_computation.154 | convolution fusion | flops 218634496 | bytes 14181376 | tf_op jit(solution)/shard_map/ghqk,gqhd->gkhd/dot_general | solution.py:197
  353.6 3.9 fusion.89
  358.0 2.0 copy.145
  361.5 3.1 fusion.68
  372.7 3.6 maximum_bitcast_fusion
  378.6 3.5 reshape_bitcast_fusion
  383.5 3.7 reshape_bitcast_fusion.1
  387.3 41.5 %reduce-scatter.19.cloned.1.call-done = f32[1,192,5376]{2,1,0:T(8,128)} async-done(((f32[1,384,5376]{2,1,0:T(8,128)}), f32[1,192,5376]{2,1,0:T(8,128)}) %reduce-scatter.19.cloned.1.call-update) | async-done | bytes 4128784 | tf_op jit(solution)/shard_map/reduce_scatter | solution.py:54
  428.8 100.9 %reduce-scatter.17.cloned.1.call-done = f32[1,192,5376]{2,1,0:T(8,128)} async-done(((f32[1,384,5376]{2,1,0:T(8,128)}), f32[1,192,5376]{2,1,0:T(8,128)}) %reduce-scatter.17.cloned.1.call-update) | async-done | bytes 4128784 | tf_op jit(solution)/shard_map/reduce_scatter | solution.py:54
  529.7 2.0 fusion.83
  531.8 2.7 fusion.170
  534.5 9.0 %reduce-scatter.31.cloned.1.call-done = f32[192,1]{1,0:T(8,128)} async-done(((f32[384,1]{1,0:T(8,128)}), f32[192,1]{1,0:T(8,128)}) %reduce-scatter.31.cloned.1.call-update) | async-done | bytes 784
  544.5 12.7 %reduce-scatter.29.cloned.1.call-done = f32[192,1]{1,0:T(8,128)} async-done(((f32[384,1]{1,0:T(8,128)}), f32[192,1]{1,0:T(8,128)}) %reduce-scatter.29.cloned.1.call-update) | async-done | bytes 784
  558.1 43.1 %reduce-scatter.27.cloned.1.call-done = f32[2880,1]{1,0:T(8,128)} async-done(((f32[5760,1]{1,0:T(8,128)}), f32[2880,1]{1,0:T(8,128)}) %reduce-scatter.27.cloned.1.call-update) | async-done | bytes 11536
  603.0 42.2 %reduce-scatter.25.cloned.1.call-done = f32[2880,1]{1,0:T(8,128)} async-done(((f32[5760,1]{1,0:T(8,128)}), f32[2880,1]{1,0:T(8,128)}) %reduce-scatter.25.cloned.1.call-update) | async-done | bytes 11536
  647.0 64.5 %all-reduce.2 = (f32[1,2880]{1,0:T(1,128)S(1)}, f32[1,2880]{1,0:T(1,128)S(1)}, f32[1,192]{1,0:T(1,128)S(1)}, f32[1,192]{1,0:T(1,128)S(1)}) all-reduce(f32[1,2880]{1,0:T(1,128)S(1)} %copy.164, f32[1,2880]{1,0:T(1,128)S(1)} %copy.162, f32[1,192]{1,0:T(1,128)S(1)} %copy.168, ...), channel_id=1, replica_groups=mesh['dp'=16,'fsdp'=2] {'dp'}, use_global_device_ids=true, to_apply=%region_55.56 | all-reduce | flops 6144 | bytes 49152 | tf_op jit(solution)/shard_map/psum | solution.py:59
  712.9 140.6 %all-reduce.7.cloned.1.call-done = (f32[1,192,5376]{2,1,0:T(8,128)}, f32[1,192,5376]{2,1,0:T(8,128)}, f32[1,768,384]{2,1,0:T(8,128)}, f32[1,768,384]{2,1,0:T(8,128)}) async-done(((f32[1,192,5376]{2,1,0:T(8,128)}, f32[1,192,5376]{2,1,0:T(8,128)}, f32[1,768,384]{2,1,0:T(8,128)}, f32[1,768,384]{2,1,0:T(8,128)}), (f32[1,192,5376]{2,1,0:T(8,128)}, f32[1,192,5376]{2,1,0:T(8,128)}, f32[1,768,384]{2,1,0:T(8,128)}, ...) | async-done | bytes 10616848 | tf_op jit(solution)/shard_map/psum | solution.py:59
  854.9 4.6 constant_dynamic-update-slice_fusion.13
  859.6 2.4 constant_dynamic-update-slice_fusion.12
  862.2 9.4 %fusion.198 = (bf16[2,768,384]{2,1,0:T(8,128)(2,1)}, f32[2,768,384]{2,1,0:T(8,128)}, f32[2,768,384]{2,1,0:T(8,128)}, f32[2,768,384]{2,1,0:T(8,128)}, f32[2,768,384]{2,1,0:T(8,128)}) fusion(f32[2,768,384]{2,1,0:T(8,128)S(1)} %copy-done.11, f32[2,768,384]{2,1,0:T(8,128)S(1)} %constant_dynamic-update-slice_fusion.14, f32[2,768,384]{2,1,0:T(8,128)} %param.26, ...), kind=kLoop, calls=%fused_computation.310 | loop fusion | flops 10027008 | bytes 20054016 | tf_op jit(solution)/shard_map/convert_element_type | solution.py:345
  871.6 21.6 %fusion.199 = (bf16[2,192,5376]{2,1,0:T(8,128)(2,1)}, f32[2,192,5376]{2,1,0:T(8,128)}, f32[2,192,5376]{2,1,0:T(8,128)}, f32[2,192,5376]{2,1,0:T(8,128)}, f32[2,192,5376]{2,1,0:T(8,128)}) fusion(f32[2,192,5376]{2,1,0:T(8,128)S(1)} %bitcast.199, f32[2,192,5376]{2,1,0:T(8,128)} %constant_dynamic-update-slice_fusion.12, f32[2,192,5376]{2,1,0:T(8,128)} %param.25, ...), kind=kLoop, calls=%fused_computation.311 | loop fusion | flops 35094528 | bytes 70189056 | tf_op jit(solution)/shard_map/convert_element_type | solution.py:340
  (321 shorter events, 76.8 us)
Async XLA Ops:
  7.2 65.1 %all-gather.11.cloned.1.call-start = ((), (), s32[]{:S(2)}) async-start(), calls=%async_computation.12 | async-start | bytes 6193152 | tf_op jit(solution)/shard_map/all_gather | solution.py:262
  13.3 117.2 %all-gather.15.cloned.1.call-start = ((), (), s32[]{:S(2)}) async-start(), calls=%async_computation.14 | async-start | bytes 6193152 | tf_op jit(solution)/shard_map/all_gather | solution.py:262
  14.0 154.1 %all-gather.13.cloned.1.call-start = ((), (), s32[]{:S(2)}) async-start(), calls=%async_computation.13 | async-start | bytes 1769472 | tf_op jit(solution)/shard_map/all_gather | solution.py:265
  15.0 1.9 copy-start.57
  15.1 1.9 copy-start.69
  15.1 14.5 %copy-start.68 = (s32[4,2]{0,1:T(2,128)S(1)}, s32[4,2]{0,1:T(2,128)}, u32[]{:S(2)}) copy-start(s32[4,2]{0,1:T(2,128)} %param.16) | copy-start | bytes 100
  15.1 14.6 %copy-start.2 = (bf16[4,256,384]{2,1,0:T(8,128)(2,1)S(1)}, bf16[4,256,384]{2,1,0:T(8,128)(2,1)}, u32[]{:S(2)}) copy-start(bf16[4,256,384]{2,1,0:T(8,128)(2,1)} %param.14) | copy-start | bytes 2359300
  15.1 57.2 %copy-start.61 = (bf16[4,384]{1,0:T(4,128)(2,1)S(1)}, bf16[4,384]{1,0:T(4,128)(2,1)}, u32[]{:S(2)}) copy-start(bf16[4,384]{1,0:T(4,128)(2,1)} %param.15) | copy-start | bytes 9220
  16.3 201.1 %all-gather.17.cloned.1.call-start = ((), (), s32[]{:S(2)}) async-start(), calls=%async_computation.15 | async-start | bytes 1769472 | tf_op jit(solution)/shard_map/all_gather | solution.py:265
  16.8 370.4 %reduce-scatter.23.cloned.1.call-start = ((), (), s32[]{:S(2)}) async-start(), calls=%async_computation.11 | async-start | bytes 3538944 | tf_op jit(solution)/shard_map/reduce_scatter | solution.py:55
  29.9 102.8 %copy-start.53 = (f32[4,256]{1,0:T(4,128)}, f32[4,256]{1,0:T(4,128)S(1)}, u32[]{:S(2)}) copy-start(f32[4,256]{1,0:T(4,128)S(1)} %broadcast_multiply_fusion.6) | copy-start | bytes 12292
  30.3 41.9 %copy-start.62 = (f32[4,256]{1,0:T(4,128)}, f32[4,256]{1,0:T(4,128)S(1)}, u32[]{:S(2)}) copy-start(f32[4,256]{1,0:T(4,128)S(1)} %fusion.67) | copy-start | bytes 12292
  30.4 102.3 %copy-start.59 = (f32[4,256]{1,0:T(4,128)}, f32[4,256]{1,0:T(4,128)S(1)}, u32[]{:S(2)}) copy-start(f32[4,256]{1,0:T(4,128)S(1)} %fusion.174) | copy-start | bytes 12292
  74.1 63.5 %copy-start.55 = (f32[4,384]{1,0:T(4,128)}, f32[4,384]{1,0:T(4,128)S(1)}, u32[]{:S(2)}) copy-start(f32[4,384]{1,0:T(4,128)S(1)} %get-tuple-element.112) | copy-start | bytes 18436
  150.0 3.4 copy-start.31
  153.4 2.7 copy-start.77
  153.4 2.7 copy-start.79
  156.9 1.9 copy-start.14
  193.2 4.5 copy-start.35
  197.7 2.7 copy-start.78
  201.2 1.9 copy-start.16
  205.7 6.5 copy-start.45
  205.8 8.2 copy-start.49
  212.3 1.7 copy-start.75
  217.3 170.0 %reduce-scatter.21.cloned.1.call-start = ((), (), s32[]{:S(2)}) async-start(), calls=%async_computation.10 | async-start | bytes 3538944 | tf_op jit(solution)/shard_map/reduce_scatter | solution.py:55
  224.9 4.1 copy-start.70
  224.9 4.1 copy-start.1
  229.0 2.2 copy-start.76
  233.1 2.0 copy-start.24
  275.5 4.2 copy-start.50
  275.5 4.2 copy-start.52
  281.5 4.2 copy-start.19
  281.5 4.2 copy-start.25
  284.7 1.9 copy-start.9
  286.6 3.3 copy-start.74
  293.2 135.7 %reduce-scatter.19.cloned.1.call-start = ((), (), s32[]{:S(2)}) async-start(), calls=%async_computation.9 | async-start | bytes 12386304 | tf_op jit(solution)/shard_map/reduce_scatter | solution.py:54
  299.9 2.2 copy-start.71
  307.1 222.6 %reduce-scatter.17.cloned.1.call-start = ((), (), s32[]{:S(2)}) async-start(), calls=%async_computation.8 | async-start | bytes 12386304 | tf_op jit(solution)/shard_map/reduce_scatter | solution.py:54
  315.9 4.0 copy-start.72
  320.5 1.9 copy-start.23
  324.2 3.4 copy-start.32
  327.7 3.7 copy-start.30
  327.7 3.7 copy-start.80
  331.4 10.5 %copy-start.28 = (bf16[4,256,1,6,64]{1,0,4,3,2:T(4,128)(2,1)S(1)}, bf16[4,256,1,6,64]{1,0,4,3,2:T(4,128)(2,1)}, u32[]{:S(2)}) copy-start(bf16[4,256,1,6,64]{1,0,4,3,2:T(4,128)(2,1)} %copy-done.27) | copy-start | bytes 2359300
  341.9 11.7 %copy-start.37 = (bf16[4,256,6,64]{1,0,3,2:T(4,128)(2,1)S(1)}, bf16[4,256,6,64]{1,0,3,2:T(4,128)(2,1)}, u32[]{:S(2)}) copy-start(bf16[4,256,6,64]{1,0,3,2:T(4,128)(2,1)} %copy-done.36) | copy-start | bytes 2359300
  353.6 4.0 copy-start.51
  361.4 3.2 copy-start.63
  361.4 3.2 copy-start.60
  361.5 4.2 copy-start.22
  366.0 1.8 copy-start.15
  369.1 2.1 copy-start.73
  376.3 167.2 %reduce-scatter.31.cloned.1.call-start = ((), (), s32[]{:S(2)}) async-start(), calls=%async_computation.19 | async-start | bytes 294912
  382.1 175.1 %reduce-scatter.29.cloned.1.call-start = ((), (), s32[]{:S(2)}) async-start(), calls=%async_computation.18 | async-start | bytes 294912
  382.7 218.5 %reduce-scatter.27.cloned.1.call-start = ((), (), s32[]{:S(2)}) async-start(), calls=%async_computation.17 | async-start | bytes 4423680
  383.4 261.8 %reduce-scatter.25.cloned.1.call-start = ((), (), s32[]{:S(2)}) async-start(), calls=%async_computation.16 | async-start | bytes 4423680
  387.2 466.3 %all-reduce.7.cloned.1.call-start = ((), (), s32[]{:S(2)}) async-start(), calls=%async_computation.20 | async-start | bytes 21233664 | tf_op jit(solution)/shard_map/psum | solution.py:59
  531.8 180.4 %copy-start.58 = (f32[2,2880]{1,0:T(2,128)S(1)}, f32[2,2880]{1,0:T(2,128)}, u32[]{:S(2)}) copy-start(f32[2,2880]{1,0:T(2,128)} %param.21) | copy-start | bytes 69124
  531.8 180.4 %copy-start.64 = (f32[2,2880]{1,0:T(2,128)S(1)}, f32[2,2880]{1,0:T(2,128)}, u32[]{:S(2)}) copy-start(f32[2,2880]{1,0:T(2,128)} %param.27) | copy-start | bytes 69124
  531.8 180.4 %copy-start.65 = (f32[2,2880]{1,0:T(2,128)S(1)}, f32[2,2880]{1,0:T(2,128)}, u32[]{:S(2)}) copy-start(f32[2,2880]{1,0:T(2,128)} %param.24) | copy-start | bytes 69124
  854.8 4.6 copy-start.38
  854.9 4.7 copy-start.26
  859.5 2.7 copy-start.11
  859.5 12.0 %slice-start = ((s8[8257536]{0:T(1024)(128)(4,1)}), s8[4194304]{0:T(1024)(128)(4,1)S(1)}, s32[]{:S(2)}) async-start(s8[8257536]{0:T(1024)(128)(4,1)} %bitcast.198), calls=%async_computation.21 | async-start | bytes 8388608
  862.2 9.4 %slice-start.1 = ((s8[8257536]{0:T(1024)(128)(4,1)}), s8[4063232]{0:T(1024)(128)(4,1)S(1)}, s32[]{:S(2)}) async-start(s8[8257536]{0:T(1024)(128)(4,1)} %bitcast.198), calls=%async_computation.22 | async-start | bytes 8126464
  (32 other events, 37.5 us)
Sparse Core Ops, SparseCore 0:
  13.4 58.8 all-gather.10
  74.4 55.9 all-gather.14
  132.5 22.7 all-gather.12
  157.3 22.7 all-gather.16
  217.4 34.6 reduce-scatter.22
  293.3 34.7 reduce-scatter.20
  331.0 97.8 reduce-scatter.18
  431.8 97.8 reduce-scatter.16
  532.5 10.9 reduce-scatter.30
  546.2 10.9 reduce-scatter.28
  560.0 41.1 reduce-scatter.26
  604.0 41.1 reduce-scatter.24
  649.2 204.2 all-reduce.6
where the time goes:
time: 911 us; the launch traced here: 900 us
  waiting for transfers between devices  491 us (54%)
  matrix products  153 us (17%)
  local copies, waits for them, and re-layouts  93.9 us (10%)
  blocking collectives  74.3 us (8%)
  other arithmetic  70.8 us (8%)
  between operations  16.8 us (2%)
    reduce_scatter x2, waiting for transfers between devices, reduce_grads(): lax.psum_scatter(grad_entry, 'fsdp', scatter_dimension=1, tiled=True)  142 us
    psum x1, waiting for transfers between devices, reduce_grads(): lax.psum((owner_grads[0], owner_grads[1], owner_grads[2], owner_grads[3])...  141 us
    unnamed x17, waiting for transfers between devices  109 us
    all_gather x2, waiting for transfers between devices, per_device(): lax.all_gather(entry_master[layer_index].astype(jnp.bfloat16), 'fsdp', ax...  98.1 us
    dot_general x30, matrix products, matmul(): return jnp.dot(left, right, preferred_element_type=jnp.float32)  87.3 us
    psum x1, blocking collectives, reduce_grads(): lax.psum((owner_grads[0], owner_grads[1], owner_grads[2], owner_grads[3])...  64.5 us
    unnamed x203, local copies, waits for them, and re-layouts  49.4 us
    dot_general x2, matrix products, block_backward(): jnp.einsum('ghqk,gqhd->gkhd', grad_scores, queries, preferred_element_typ...  23.2 us
  transfers between devices with their start and end apart: 13, of which 9 were waited for; matrix products, arithmetic and copies ran while one was open for 27% of the time, Pallas kernels for 0%

commit v1 on v0

--- a/solution.py
+++ b/solution.py
@@ -19,6 +19,18 @@
 adam_eps = 1e-08
 learn_rate = 0.02
 decay_rate = 0.1
+
+
+def collect(array, axis, dim):
+    ways, here = (lax.axis_size(axis), lax.axis_index(axis))
+    grown, reach = (array, 1)
+    while reach < ways:
+        theirs = lax.ppermute(grown, axis, [(d, d ^ reach) for d in range(ways)])
+        mine_first = jnp.concatenate([grown, theirs], axis=dim)
+        theirs_first = jnp.concatenate([theirs, grown], axis=dim)
+        grown = jnp.where(here & reach == 0, mine_first, theirs_first)
+        reach = 2 * reach
+    return grown
 
 
 def matmul(left, right):
@@ -259,9 +271,7 @@
     residual = tokens.astype(jnp.float32)
     for layer_index in range(LAYERS):
         gathered = (
-            lax.all_gather(
-                entry_master[layer_index].astype(jnp.bfloat16), "fsdp", axis=0, tiled=True
-            ),
+            collect(entry_master[layer_index].astype(jnp.bfloat16), "fsdp", 0),
             lax.all_gather(
                 exit_master[layer_index].astype(jnp.bfloat16), "fsdp", axis=0, tiled=True
             ),

time: 911 us -> 1000 us (1.098)
  blocking collectives: 74.3 us -> 225 us
  waiting for transfers between devices: 491 us -> 358 us
  matrix products: 153 us -> 182 us
  local copies, waits for them, and re-layouts: 93.9 us -> 120 us
  other arithmetic: 70.8 us -> 90.3 us
    unnamed x1, blocking collectives: 9.8 us -> 160 us
    all_gather x2, waiting for transfers between devices: 98.1 us -> 0.02 us  [per_device(): lax.all_gather(entry_master[layer_index].astype(jnp.bfloat16), 'fsdp', ax...]
    dot_general x30 -> x38, matrix products: 87.3 us -> 113 us  [matmul(): return jnp.dot(left, right, preferred_element_type=jnp.float32)]
    reduce_scatter x2, waiting for transfers between devices: 142 us -> 118 us  [reduce_grads(): lax.psum_scatter(grad_entry, 'fsdp', scatter_dimension=1, tiled=True)]
    reshape x2 -> x4, local copies, waits for them, and re-layouts: 11.2 us -> 22.6 us  [block_forward(): projected = projected.reshape(images, SLOTS, 3, HEADS, HEAD_DIM)]
    unnamed x17, waiting for transfers between devices: 109 us -> 99.2 us
    unnamed x203 -> x243, local copies, waits for them, and re-layouts: 49.4 us -> 51 us
  transfers between devices with their start and end apart: 13 -> 15, of which waited for: 9 -> 6; matrix products, arithmetic and copies ran while one was open for 27% -> 29% of each run, Pallas kernels for 0% -> 0%
where the time goes in v1:
time: 1000 us; the launch traced here: 996 us
  waiting for transfers between devices  358 us (36%)
  blocking collectives  225 us (22%)
  matrix products  182 us (18%)
  local copies, waits for them, and re-layouts  120 us (12%)
  other arithmetic  90.3 us (9%)
  between operations  17.2 us (2%)
    unnamed x1, blocking collectives  160 us
    psum x1, waiting for transfers between devices, reduce_grads(): lax.psum((owner_grads[0], owner_grads[1], owner_grads[2], owner_grads[3])...  140 us
    reduce_scatter x2, waiting for transfers between devices, reduce_grads(): lax.psum_scatter(grad_entry, 'fsdp', scatter_dimension=1, tiled=True)  118 us
    dot_general x38, matrix products, matmul(): return jnp.dot(left, right, preferred_element_type=jnp.float32)  113 us
    unnamed x17, waiting for transfers between devices  99.2 us
    psum x1, blocking collectives, reduce_grads(): lax.psum((owner_grads[0], owner_grads[1], owner_grads[2], owner_grads[3])...  64.9 us
    unnamed x243, local copies, waits for them, and re-layouts  51 us
    dot_general x2, matrix products, block_backward(): jnp.einsum('ghqk,gqhd->gkhd', grad_scores, queries, preferred_element_typ...  22.8 us
  transfers between devices with their start and end apart: 15, of which 6 were waited for; matrix products, arithmetic and copies ran while one was open for 29% of the time, Pallas kernels for 0%

profile of v1, /device:TPU:0, one launch (start us, length us, event | category | flops | bytes accessed | tf_op | source)
XLA Modules:
  0.0 995.9 jit_solution(8832561750148185453)
XLA Ops:
  7.2 3.8 convert.48
  11.0 3.6 fusion.273
  17.6 3.0 collective-permute-start
  23.4 160.3 %all-reduce.4 = (bf16[5760]{0:T(1024)(128)(2,1)S(1)}, bf16[5760]{0:T(1024)(128)(2,1)S(1)}) all-reduce(bf16[5760]{0:T(1024)(128)(2,1)S(1)} %dynamic-update-slice, bf16[5760]{0:T(1024)(128)(2,1)S(1)} %dynamic-update-slice.1), channel_id=2, replica_groups=mesh['dp'=16,'fsdp'=2] {'fsdp'}, use_global_device_ids=true, to_apply=%add | all-reduce | flops 11520 | bytes 46080
  185.4 4.8 maximum_select_fusion
  192.2 2.7 maximum_select_fusion.1
  203.4 4.0 fusion.46
  207.4 4.3 copy.149
  211.7 5.6 reshape.438
  217.3 2.6 fusion.277
  219.9 4.0 fusion.49
  224.0 4.3 copy.175
  228.2 5.6 reshape.460
  233.8 2.5 fusion.274
  237.5 2.4 fusion.282
  248.2 2.8 convolution_add_fusion.8
  254.5 6.3 fusion.152
  260.8 3.9 fusion.270
  266.6 4.0 fusion.48
  270.6 4.3 copy.161
  274.9 5.8 reshape.451
  280.7 2.4 fusion.275
  297.7 6.4 multiply_convert_fusion.1
  304.1 8.5 convert_reduce_fusion
  312.6 3.9 fusion.187
  321.0 2.7 convert_reduce_fusion.6
  328.0 5.3 convolution_bitcast_fusion
  334.4 4.9 fusion.203
  339.3 11.4 %fusion.130 = bf16[4,256,1,6,64]{1,4,3,0,2:T(8,128)(2,1)} fusion(f32[4,6,256,256]{2,3,1,0:T(8,128)} %fusion.203, pred[4,256]{1,0:T(4,128)(4,1)S(1)} %get-tuple-element.137, bf16[4,256,1,6,64]{1,0,4,3,2:T(4,128)(2,1)S(1)} %copy-done.39, f32[4,6,256,256]{2,3,1,0:T(8,128)} %copy-done.95, f32[4,6,256]{2,1,0:T(8,128)S(1)} %get-tuple-element.142), kind=kOutput, calls=%fused_computation.207 | convolution fusion | flops 218634496 | bytes 14181376 | tf_op jit(solution)/shard_map/ghqk,gkhd->gqhd/dot_general | solution.py:206
  350.7 11.3 %fusion.135 = bf16[4,256,1,6,64]{1,4,3,0,2:T(8,128)(2,1)} fusion(f32[4,6,256,256]{2,3,1,0:T(8,128)} %fusion.203, pred[4,256]{1,0:T(4,128)(4,1)S(1)} %get-tuple-element.137, bf16[4,256,1,6,64]{1,0,4,3,2:T(4,128)(2,1)S(1)} %copy-done.37, f32[4,6,256,256]{2,3,1,0:T(8,128)} %copy-done.95, f32[4,6,256]{2,1,0:T(8,128)S(1)} %get-tuple-element.142), kind=kOutput, calls=%fused_computation.208 | convolution fusion | flops 218634496 | bytes 14181376 | tf_op jit(solution)/shard_map/ghqk,gqhd->gkhd/dot_general | solution.py:209
  362.0 4.1 fusion.124
  367.9 3.1 multiply_reduce_fusion.9
  372.9 3.2 multiply_reduce_fusion.4
  376.9 6.3 multiply_convert_fusion
  384.8 3.3 convolution_bitcast_fusion.1
  388.6 3.7 copy.191
  398.9 3.6 maximum_bitcast_fusion.1
  402.6 4.3 fusion.47
  406.9 4.3 copy.155
  411.1 5.6 reshape.444
  416.7 2.5 fusion.276
  426.5 6.0 convert_reduce_fusion.1
  432.5 4.1 fusion.183
  440.7 3.1 convert_reduce_fusion.8
  447.3 3.7 fusion.205
  451.0 10.7 %fusion.140 = bf16[4,256,1,6,64]{1,4,3,0,2:T(8,128)(2,1)S(1)} fusion(f32[4,6,256,256]{2,3,1,0:T(8,128)} %fusion.205, pred[4,256]{1,0:T(4,128)(4,1)S(1)} %get-tuple-element.137, bf16[4,256,1,6,64]{1,0,4,3,2:T(4,128)(2,1)S(1)} %copy-done.33, f32[4,6,256,256]{2,3,1,0:T(8,128)} %copy-done.94, f32[4,6,256]{2,1,0:T(8,128)S(1)} %copy-done.97), kind=kOutput, calls=%fused_computation.209 | convolution fusion | flops 218634496 | bytes 14181376 | tf_op jit(solution)/shard_map/ghqk,gkhd->gqhd/dot_general | solution.py:206
  461.8 11.5 %fusion.145 = bf16[4,256,1,6,64]{1,4,3,0,2:T(8,128)(2,1)} fusion(f32[4,6,256,256]{2,3,1,0:T(8,128)} %fusion.205, pred[4,256]{1,0:T(4,128)(4,1)S(1)} %get-tuple-element.137, bf16[4,256,1,6,64]{1,0,4,3,2:T(4,128)(2,1)S(1)} %copy-done.31, f32[4,6,256,256]{2,3,1,0:T(8,128)} %copy-done.94, f32[4,6,256]{2,1,0:T(8,128)S(1)} %copy-done.97), kind=kOutput, calls=%fused_computation.210 | convolution fusion | flops 218634496 | bytes 14181376 | tf_op jit(solution)/shard_map/ghqk,gqhd->gkhd/dot_general | solution.py:209
  473.3 4.2 fusion.127
  481.5 3.1 fusion.103
  492.9 3.6 maximum_bitcast_fusion
  498.9 3.5 reshape_bitcast_fusion
  503.8 3.5 reshape_bitcast_fusion.1
  507.5 17.3 %reduce-scatter.19.cloned.1.call-done = f32[1,192,5376]{2,1,0:T(8,128)} async-done(((f32[1,384,5376]{2,1,0:T(8,128)}), f32[1,192,5376]{2,1,0:T(8,128)}) %reduce-scatter.19.cloned.1.call-update) | async-done | bytes 4128784 | tf_op jit(solution)/shard_map/reduce_scatter | solution.py:66
  524.7 100.9 %reduce-scatter.17.cloned.1.call-done = f32[1,192,5376]{2,1,0:T(8,128)} async-done(((f32[1,384,5376]{2,1,0:T(8,128)}), f32[1,192,5376]{2,1,0:T(8,128)}) %reduce-scatter.17.cloned.1.call-update) | async-done | bytes 4128784 | tf_op jit(solution)/shard_map/reduce_scatter | solution.py:66
  629.5 2.7 fusion.225
  633.4 5.5 fusion.153
  641.0 12.0 %reduce-scatter.29.cloned.1.call-done = f32[192,1]{1,0:T(8,128)} async-done(((f32[384,1]{1,0:T(8,128)}), f32[192,1]{1,0:T(8,128)}) %reduce-scatter.29.cloned.1.call-update) | async-done | bytes 784
  654.0 43.1 %reduce-scatter.27.cloned.1.call-done = f32[2880,1]{1,0:T(8,128)} async-done(((f32[5760,1]{1,0:T(8,128)}), f32[2880,1]{1,0:T(8,128)}) %reduce-scatter.27.cloned.1.call-update) | async-done | bytes 11536
  698.9 42.2 %reduce-scatter.25.cloned.1.call-done = f32[2880,1]{1,0:T(8,128)} async-done(((f32[5760,1]{1,0:T(8,128)}), f32[2880,1]{1,0:T(8,128)}) %reduce-scatter.25.cloned.1.call-update) | async-done | bytes 11536
  742.9 64.9 %all-reduce.2 = (f32[1,2880]{1,0:T(1,128)S(1)}, f32[1,2880]{1,0:T(1,128)S(1)}, f32[1,192]{1,0:T(1,128)S(1)}, f32[1,192]{1,0:T(1,128)S(1)}) all-reduce(f32[1,2880]{1,0:T(1,128)S(1)} %copy.210, f32[1,2880]{1,0:T(1,128)S(1)} %copy.208, f32[1,192]{1,0:T(1,128)S(1)} %copy.214, ...), channel_id=1, replica_groups=mesh['dp'=16,'fsdp'=2] {'dp'}, use_global_device_ids=true, to_apply=%region_63.64 | all-reduce | flops 6144 | bytes 49152 | tf_op jit(solution)/shard_map/psum | solution.py:71
  809.2 140.2 %all-reduce.7.cloned.1.call-done = (f32[1,192,5376]{2,1,0:T(8,128)}, f32[1,192,5376]{2,1,0:T(8,128)}, f32[1,768,384]{2,1,0:T(8,128)}, f32[1,768,384]{2,1,0:T(8,128)}) async-done(((f32[1,192,5376]{2,1,0:T(8,128)}, f32[1,192,5376]{2,1,0:T(8,128)}, f32[1,768,384]{2,1,0:T(8,128)}, f32[1,768,384]{2,1,0:T(8,128)}), (f32[1,192,5376]{2,1,0:T(8,128)}, f32[1,192,5376]{2,1,0:T(8,128)}, f32[1,768,384]{2,1,0:T(8,128)}, ...) | async-done | bytes 10616848 | tf_op jit(solution)/shard_map/psum | solution.py:71
  950.8 4.6 constant_dynamic-update-slice_fusion.13
  958.1 9.4 fusion.268
  967.5 21.6 %fusion.269 = (bf16[2,192,5376]{2,1,0:T(8,128)(2,1)}, f32[2,192,5376]{2,1,0:T(8,128)}, f32[2,192,5376]{2,1,0:T(8,128)}, f32[2,192,5376]{2,1,0:T(8,128)}, f32[2,192,5376]{2,1,0:T(8,128)}) fusion(f32[2,192,5376]{2,1,0:T(8,128)S(1)} %bitcast.268, f32[2,192,5376]{2,1,0:T(8,128)} %constant_dynamic-update-slice_fusion.12, f32[2,192,5376]{2,1,0:T(8,128)} %param.25, ...), kind=kLoop, calls=%fused_computation.416 | loop fusion | flops 35094528 | bytes 70189056 | tf_op jit(solution)/shard_map/convert_element_type | solution.py:350
  (401 shorter events, 115.8 us)
Async XLA Ops:
  7.2 190.7 %all-gather.17.cloned.1.call-start = ((), (), s32[]{:S(2)}) async-start(), calls=%async_computation.15 | async-start | bytes 6193152 | tf_op jit(solution)/shard_map/all_gather | solution.py:293
  14.6 185.1 %all-gather.15.cloned.1.call-start = ((), (), s32[]{:S(2)}) async-start(), calls=%async_computation.14 | async-start | bytes 6193152 | tf_op jit(solution)/shard_map/all_gather | solution.py:293
  15.4 239.1 %all-gather.11.cloned.1.call-start = ((), (), s32[]{:S(2)}) async-start(), calls=%async_computation.12 | async-start | bytes 1769472 | tf_op jit(solution)/shard_map/all_gather | solution.py:275
  16.4 5.1 copy-start.67
  16.4 5.2 copy-start.89
  16.4 167.6 %copy-start = (bf16[4,256,384]{2,1,0:T(8,128)(2,1)S(1)}, bf16[4,256,384]{2,1,0:T(8,128)(2,1)}, u32[]{:S(2)}) copy-start(bf16[4,256,384]{2,1,0:T(8,128)(2,1)} %param.14) | copy-start | bytes 2359300
  16.4 168.3 %copy-start.88 = (s32[4,2]{0,1:T(2,128)S(1)}, s32[4,2]{0,1:T(2,128)}, u32[]{:S(2)}) copy-start(s32[4,2]{0,1:T(2,128)} %param.16) | copy-start | bytes 100
  17.6 286.5 %all-gather.13.cloned.1.call-start = ((), (), s32[]{:S(2)}) async-start(), calls=%async_computation.13 | async-start | bytes 1769472 | tf_op jit(solution)/shard_map/all_gather | solution.py:275
  17.6 167.7 %collective-permute-start = (bf16[192,5376]{1,0:T(8,128)(2,1)}, bf16[192,5376]{1,0:T(8,128)(2,1)}, u32[]{:S(2)}, u32[]{:S(2)}) collective-permute-start(bf16[192,5376]{1,0:T(8,128)(2,1)} %get-tuple-element.85), channel_id=1, source_target_pairs={{0,1},{1,0},{2,3},{3,2},{4,5},{5,4},{6,7},{7,6},{8,9},{9,8},{10,11... | collective-permute-start | bytes 6193160 | tf_op jit(solution)/shard_map/ppermute | solution.py:28
  20.7 171.5 %collective-permute-start.1 = (bf16[192,5376]{1,0:T(8,128)(2,1)}, bf16[192,5376]{1,0:T(8,128)(2,1)}, u32[]{:S(2)}, u32[]{:S(2)}) collective-permute-start(bf16[192,5376]{1,0:T(8,128)(2,1)} %get-tuple-element.86), channel_id=1, source_target_pairs={{0,1},{1,0},{2,3},{3,2},{4,5},{5,4},{6,7},{7,6},{8,9},{9,8},{10,11... | collective-permute-start | bytes 6193160 | tf_op jit(solution)/shard_map/ppermute | solution.py:28
  20.8 486.7 %reduce-scatter.23.cloned.1.call-start = ((), (), s32[]{:S(2)}) async-start(), calls=%async_computation.11 | async-start | bytes 3538944 | tf_op jit(solution)/shard_map/reduce_scatter | solution.py:67
  183.8 70.7 %copy-start.82 = (f32[384]{0:T(512)}, f32[384]{0:T(512)S(1)}, u32[]{:S(2)}) copy-start(f32[384]{0:T(512)S(1)} %get-tuple-element.35) | copy-start | bytes 4612
  184.0 120.1 %copy-start.85 = (f32[1536]{0:T(1024)}, f32[1536]{0:T(1024)S(1)}, u32[]{:S(2)}) copy-start(f32[1536]{0:T(1024)S(1)} %slice_reduce_fusion.4) | copy-start | bytes 18436
  184.3 17.3 %copy-start.63 = (f32[4,256]{1,0:T(4,128)}, f32[4,256]{1,0:T(4,128)S(1)}, u32[]{:S(2)}) copy-start(f32[4,256]{1,0:T(4,128)S(1)} %broadcast_multiply_fusion.8) | copy-start | bytes 12292
  185.4 16.2 %copy-start.69 = (f32[4,256]{1,0:T(4,128)}, f32[4,256]{1,0:T(4,128)S(1)}, u32[]{:S(2)}) copy-start(f32[4,256]{1,0:T(4,128)S(1)} %fusion.229) | copy-start | bytes 12292
  185.4 4.8 copy-start.61
  185.4 6.8 copy-start.15
  199.7 7.7 copy-start.65
  199.7 61.1 %copy-start.71 = (f32[4,384]{1,0:T(4,128)}, f32[4,384]{1,0:T(4,128)S(1)}, u32[]{:S(2)}) copy-start(f32[4,384]{1,0:T(4,128)S(1)} %get-tuple-element.116) | copy-start | bytes 18436
  236.4 3.6 copy-start.34
  243.4 4.7 copy-start.16
  283.1 4.4 copy-start.40
  312.6 3.9 copy-start.90
  333.3 6.0 copy-start.39
  333.3 174.1 %reduce-scatter.21.cloned.1.call-start = ((), (), s32[]{:S(2)}) async-start(), calls=%async_computation.10 | async-start | bytes 3538944 | tf_op jit(solution)/shard_map/reduce_scatter | solution.py:67
  339.3 11.4 %copy-start.37 = (bf16[4,256,1,6,64]{1,0,4,3,2:T(4,128)(2,1)S(1)}, bf16[4,256,1,6,64]{1,0,4,3,2:T(4,128)(2,1)}, u32[]{:S(2)}) copy-start(bf16[4,256,1,6,64]{1,0,4,3,2:T(4,128)(2,1)} %copy-done.36) | copy-start | bytes 2359300
  350.7 11.3 %copy-start.42 = (bf16[4,256,6,64]{1,0,3,2:T(4,128)(2,1)S(1)}, bf16[4,256,6,64]{1,0,3,2:T(4,128)(2,1)}, u32[]{:S(2)}) copy-start(bf16[4,256,6,64]{1,0,3,2:T(4,128)(2,1)} %reshape.457) | copy-start | bytes 2359300
  362.0 4.1 copy-start.56
  362.0 4.1 copy-start.58
  367.9 4.1 copy-start.23
  367.9 4.1 copy-start.29
  367.9 4.1 copy-start.47
  372.9 3.2 copy-start.2
  376.1 7.1 copy-start.59
  376.9 6.3 copy-start.50
  388.1 136.6 %reduce-scatter.19.cloned.1.call-start = ((), (), s32[]{:S(2)}) async-start(), calls=%async_computation.9 | async-start | bytes 12386304 | tf_op jit(solution)/shard_map/reduce_scatter | solution.py:66
  402.5 223.1 %reduce-scatter.17.cloned.1.call-start = ((), (), s32[]{:S(2)}) async-start(), calls=%async_computation.8 | async-start | bytes 12386304 | tf_op jit(solution)/shard_map/reduce_scatter | solution.py:66
  422.6 3.9 slice-start.2
  422.6 3.9 slice-start.3
  432.5 4.1 copy-start.92
  432.5 4.1 copy-start.78
  443.8 3.4 copy-start.35
  447.3 3.7 copy-start.33
  447.3 3.7 copy-start.97
  451.0 10.8 %copy-start.31 = (bf16[4,256,1,6,64]{1,0,4,3,2:T(4,128)(2,1)S(1)}, bf16[4,256,1,6,64]{1,0,4,3,2:T(4,128)(2,1)}, u32[]{:S(2)}) copy-start(bf16[4,256,1,6,64]{1,0,4,3,2:T(4,128)(2,1)} %copy-done.30) | copy-start | bytes 2359300
  461.8 11.5 %copy-start.44 = (bf16[4,256,6,64]{1,0,3,2:T(4,128)(2,1)S(1)}, bf16[4,256,6,64]{1,0,3,2:T(4,128)(2,1)}, u32[]{:S(2)}) copy-start(bf16[4,256,6,64]{1,0,3,2:T(4,128)(2,1)} %copy-done.43) | copy-start | bytes 2359300
  473.3 4.2 copy-start.57
  481.5 4.2 copy-start.24
  496.6 143.4 %reduce-scatter.31.cloned.1.call-start = ((), (), s32[]{:S(2)}) async-start(), calls=%async_computation.19 | async-start | bytes 294912
  502.4 150.6 %reduce-scatter.29.cloned.1.call-start = ((), (), s32[]{:S(2)}) async-start(), calls=%async_computation.18 | async-start | bytes 294912
  503.0 194.1 %reduce-scatter.27.cloned.1.call-start = ((), (), s32[]{:S(2)}) async-start(), calls=%async_computation.17 | async-start | bytes 4423680
  503.8 237.4 %reduce-scatter.25.cloned.1.call-start = ((), (), s32[]{:S(2)}) async-start(), calls=%async_computation.16 | async-start | bytes 4423680
  507.4 442.0 %all-reduce.7.cloned.1.call-start = ((), (), s32[]{:S(2)}) async-start(), calls=%async_computation.20 | async-start | bytes 21233664 | tf_op jit(solution)/shard_map/psum | solution.py:71
  627.0 5.1 copy-start.76
  627.0 5.2 copy-start.77
  629.5 4.0 copy-start.86
  633.4 5.5 copy-start.75
  640.0 168.5 %copy-start.68 = (f32[2,2880]{1,0:T(2,128)S(1)}, f32[2,2880]{1,0:T(2,128)}, u32[]{:S(2)}) copy-start(f32[2,2880]{1,0:T(2,128)} %param.21) | copy-start | bytes 69124
  640.0 168.5 %copy-start.79 = (f32[2,2880]{1,0:T(2,128)S(1)}, f32[2,2880]{1,0:T(2,128)}, u32[]{:S(2)}) copy-start(f32[2,2880]{1,0:T(2,128)} %param.27) | copy-start | bytes 69124
  640.0 168.5 %copy-start.80 = (f32[2,2880]{1,0:T(2,128)S(1)}, f32[2,2880]{1,0:T(2,128)}, u32[]{:S(2)}) copy-start(f32[2,2880]{1,0:T(2,128)} %param.24) | copy-start | bytes 69124
  950.7 4.6 copy-start.46
  950.7 4.7 copy-start.26
  955.4 12.0 %slice-start = ((s8[8257536]{0:T(1024)(128)(4,1)}), s8[4194304]{0:T(1024)(128)(4,1)S(1)}, s32[]{:S(2)}) async-start(s8[8257536]{0:T(1024)(128)(4,1)} %bitcast.267), calls=%async_computation.21 | async-start | bytes 8388608
  958.1 9.4 slice-start.1
  (53 other events, 86.8 us)
Sparse Core Ops, SparseCore 0:
  14.7 103.0 all-gather.16
  120.0 79.2 all-gather.14
  201.4 24.2 all-gather.10
  227.1 22.7 all-gather.12
  333.4 35.7 reduce-scatter.22
  388.2 35.6 reduce-scatter.20
  426.9 97.8 reduce-scatter.18
  527.7 97.8 reduce-scatter.16
  628.4 10.9 reduce-scatter.30
  642.1 10.9 reduce-scatter.28
  655.9 41.1 reduce-scatter.26
  699.9 41.2 reduce-scatter.24
  745.1 204.2 all-reduce.6
